TPU v7x, 128 devices: a whole 4x4x4 slice. The times are simulated.
128 devices in a mesh: tm: 16 (over z_hi, x, core), height: 8 (over z_lo, y).
Axes of the slice: x: 4, y: 4, z: 4 (z_hi: 2, z_lo: 2; z = z_hi * 2 + z_lo), core: 2. Of those that a mesh axis runs over, the one named last changes fastest.
Arguments:
- coarse: bfloat16 [8, 32, 128, 256], P('height', 'tm'), may hold values from -360 to 360
- gain: float32 [256], replicated, may hold values from 0.1 to 1.9
- bias: float32 [256], replicated, may hold values from -3 to 3
- weight: bfloat16 [256, 3, 3, 3, 128], replicated, may hold values from -0.078125 to 0.078125
- cotangent: bfloat16 [8, 64, 256, 128], P(None, 'tm', 'height'), may hold values from -0.0390625 to 0.0390625
Outputs:
- decoded: bfloat16 [8, 64, 256, 128], P(None, 'tm', 'height')
- grad_weight: float32 [256, 3, 3, 3, 128], P('tm')
- grad_affine: float32 [2, 256], replicated
All inputs are finite; a program needn't handle non-finite values.
Results may differ from a plain program's by a relative error of at most 0.0051.
Values may be sent and summed in bfloat16 or wider, within the bound.
A program may use at most 64 MiB of HBM per device.

v0:
```python
import functools

import jax
import jax.numpy as jnp
from jax import lax
from jax.experimental import pallas as pl
from jax.experimental.pallas import tpu as pltpu
from jax.sharding import PartitionSpec as P

MESH = pl.DeviceIdType.MESH
F32, BF16 = jnp.float32, jnp.bfloat16
EPSILON = 1e-06
NUMBERS = 8 * 32 * 128 * 8
CHIPS, HEIGHT = 8, 8
EXTRA = (0, 3, 6)

(STATS1, STATS2, BLOCKS, COT_PAIR, COT_ROWS, COT_COLS, X_PAIR, X_ROWS, X_COLS, ALONG_X, ALONG_Y, ALONG_Z, LAST_X, LAST_Y, LAST_Z, LAST_E, GATHER, AFF1, AFF2, ROWS_ON, COLS_ON) = range(21)


def group_totals(tile):
    lane = lax.broadcasted_iota(jnp.int32, tile.shape, 1)
    for step in (1, 2, 4):
        other = jnp.where(
            (lane & step) == 0, pltpu.roll(tile, 128 - step, 1), pltpu.roll(tile, step, 1)
        )
        tile = tile + other
    return tile


def kernel(
    coarse_hbm, gain_hbm, bias_hbm, w_hbm, cot_hbm, dec, gw, aff,
    coarse, gain, bias, w, cot, fetch_sem, wc, st, sa, st1, st2, af, at, at1, at2,
    xraw, xf, xe, hc, acts, pad0, pad1, a_t,
    cpart, cedge, ce, ch, cf, s_buf,
    gx, gy, gz, rx, ry, rz, px, py, pz, qx, qy, qz, qe, ag_s, ag_r, d_buf, ssem, rsem,
):
    tm, h = lax.axis_index("tm"), lax.axis_index("height")
    core = lax.rem(tm, 2)
    t = tm // 2
    left, right = lax.rem(h + 7, 8), lax.rem(h + 1, 8)
    t_off = lax.rem(t + 7 + 2 * core, 8)
    pair = tm + 1 - 2 * core

    def others_h():
        for dz, dy in ((1, 2), (1, 1), (1, 3), (0, 2), (1, 0), (0, 1), (0, 3)):
            yield lax.rem(h // 4 + dz, 2) * 4 + lax.rem(h + dy, 4)

    def others_tm():
        for dz, dx in ((1, 2), (1, 1), (1, 3), (1, 0), (0, 2), (0, 1), (0, 3)):
            chip = lax.rem(t // 4 + dz, 2) * 4 + lax.rem(t + dx, 4)
            yield 2 * chip + core
            yield 2 * chip + 1 - core
        yield pair

    def send(src, dst, kind, to_tm, to_h):
        pltpu.make_async_remote_copy(
            src_ref=src, dst_ref=dst, send_sem=ssem.at[kind], recv_sem=rsem.at[kind],
            device_id=(to_tm, to_h), device_id_type=MESH,
        ).start()

    def arrived(kind, like):
        pltpu.make_async_copy(like, like, rsem.at[kind]).wait()

    def sent(kind, like):
        pltpu.make_async_copy(like, like, ssem.at[kind]).wait()

    pairs = ((coarse_hbm, coarse), (cot_hbm, cot), (gain_hbm, gain), (bias_hbm, bias), (w_hbm, w))
    fetches = [pltpu.make_async_copy(src, dst, fetch_sem.at[i]) for i, (src, dst) in enumerate(pairs)]
    for fetch in fetches:
        fetch.start()

    barrier = pltpu.get_barrier_semaphore()

    def greet(to_tm, to_h):
        pl.semaphore_signal(barrier, inc=1, device_id=(to_tm, to_h), device_id_type=MESH)

    for to_tm in others_tm():
        greet(to_tm, h)
    for to_h in others_h():
        greet(tm, to_h)

    greet(pair, left)
    greet(pair, right)

    @pl.loop(0, 4)
    def _(k):
        to_tm = lax.rem(t + 7 + 2 * (k // 2), 8) * 2 + lax.rem(k, 2)
        greet(to_tm, left)
        greet(to_tm, right)

    fetches[0].wait()
    x = coarse[...].astype(F32).reshape(256, 256)
    total = jnp.sum(x, axis=0, keepdims=True)
    squares = jnp.sum(x * x, axis=0, keepdims=True)
    quarters = (total[:, :128], total[:, 128:], squares[:, :128], squares[:, 128:])
    quarter = lax.rem(lax.broadcasted_iota(jnp.int32, (4, 128), 1), 4)
    mine = quarter == lax.broadcasted_iota(jnp.int32, (4, 128), 0)
    sums = group_totals(jnp.concatenate(quarters, axis=0))
    st[...] = jnp.sum(jnp.where(mine, sums, 0.0), axis=0, keepdims=True)

    pl.semaphore_wait(barrier, 32)

    for to_h in others_h():
        send(st, st1.at[h], STATS1, tm, to_h)

    for to_h in others_h():
        send(
            coarse.at[:, pl.ds(pl.multiple_of(to_h * 16, 16), 16), :],
            xraw.at[h, pl.ds(1 + 2 * core, 2)], BLOCKS, tm, to_h,
        )

    fetches[1].wait()
    send(cot, cpart, COT_PAIR, pair, h)
    send(cot.at[:, pl.ds(3 * core, 1)], cedge.at[1 - core], COT_ROWS, t_off * 2 + 1 - core, h)
    def cell(j, f):
        return pl.multiple_of((j * 8 + f) * 48, 8)

    for r in range(4):
        for f in range(8):
            cf[pl.ds(cell(1 + 4 * core + r, f) + 8, 32), :] = cot[f, r].astype(F32)
    for r in range(4):
        base = cell(1 + 4 * core + r, 0)
        ce[0, r] = cf[pl.ds(base + 8, 8, stride=48), :]
        ce[1, r] = cf[pl.ds(base + 39, 8, stride=48), :]

    for side, to_h in ((0, left), (1, right)):
        send(ce.at[side], ch.at[1 - side, pl.ds(1 + 4 * core, 4)], COT_COLS, tm, to_h)
        send(ce.at[side, pl.ds(3 * core, 1)], ch.at[1 - side, pl.ds(9 - 9 * core, 1)], COT_COLS, t_off * 2 + 1 - core, to_h)

    st1[h] = st[...]
    xraw[h, pl.ds(1 + 2 * core, 2)] = coarse[:, pl.ds(pl.multiple_of(h * 16, 16), 16), :]

    arrived(STATS1, st1.at[pl.ds(0, 7)])
    sa[...] = jnp.sum(st1[...], axis=0)

    for to_tm in others_tm():
        send(sa, st2.at[tm], STATS2, to_tm, h)

    st2[tm] = sa[...]

    arrived(BLOCKS, xraw.at[pl.ds(0, 7), pl.ds(0, 2)])
    own = xraw.at[:, pl.ds(1 + 2 * core, 2)]
    send(own, own, X_PAIR, pair, h)
    send(xraw.at[:, pl.ds(1 + 3 * core, 1)], xraw.at[:, pl.ds(5 - 5 * core, 1)], X_ROWS, t_off * 2 + 1 - core, h)

    s_buf[:, 8:10] = jnp.zeros((9, 2, 4, 16, 128), BF16)
    half_rows = ch.at[:, pl.ds(5 * core, 5)]
    arrived(COT_ROWS, cedge.at[0])
    send(cedge.at[core], cedge.at[core], ROWS_ON, pair, h)
    arrived(COT_COLS, ch.at[:, pl.ds(0, 5)])
    send(half_rows, half_rows, COLS_ON, pair, h)
    arrived(COT_PAIR, cpart)
    for r in range(4):
        for f in range(8):
            cf[pl.ds(cell(5 - 4 * core + r, f) + 8, 32), :] = cpart[f, r].astype(F32)
    arrived(ROWS_ON, cedge.at[0])
    arrived(COLS_ON, ch.at[:, pl.ds(0, 5)])
    top, bottom = t > 0, t < CHIPS - 1
    for f in range(8):
        cf[pl.ds(cell(0, f) + 8, 32), :] = jnp.where(top, cedge[0, f, 0].astype(F32), 0.0)
        cf[pl.ds(cell(9, f) + 8, 32), :] = jnp.where(bottom, cedge[1, f, 0].astype(F32), 0.0)
    for j in range(10):
        keep = (h > 0, h < HEIGHT - 1)
        if j == 0:
            keep = tuple(jnp.logical_and(k, top) for k in keep)
        if j == 9:
            keep = tuple(jnp.logical_and(k, bottom) for k in keep)
        cf[pl.ds(j * 384 + 7, 8, stride=48), :] = jnp.where(keep[0], ch[0, j], 0.0)
        cf[pl.ds(j * 384 + 40, 8, stride=48), :] = jnp.where(keep[1], ch[1, j], 0.0)

    @pl.loop(0, 8)
    def _(f):
        sums = []
        for j in range(10):
            base = cell(j, f)
            cols = [cf[pl.ds(base + 7 + i, 16, stride=2), :] for i in range(4)]
            sums.append((cols[2] + cols[3], cols[1] + cols[2], cols[0] + cols[1]))
        for b in range(3):
            for e in range(3):
                for row in range(4):
                    s_buf[b * 3 + e, f, row] = (sums[2 * row + 2 - b][e] + sums[2 * row + 3 - b][e]).astype(BF16)

    for r in range(2):
        rows = xraw[:, 1 + 2 * core + r].astype(F32).reshape(128, 256)
        for half in range(2):
            xf[half, 0:128, :] = rows[:, 128 * half : 128 * half + 128]
            for side, column in ((0, 0), (1, 15)):
                xe[side, r, :, 128 * half : 128 * half + 128] = xf.at[half][pl.ds(column, 8, stride=16), :]
    for side, to_h in ((0, left), (1, right)):
        send(xe.at[side], hc.at[1 - side, pl.ds(1 + 2 * core, 2)], X_COLS, tm, to_h)
        send(xe.at[side, pl.ds(1 - core, 1)], hc.at[1 - side, pl.ds(2 + core, 1)], X_COLS, pair, to_h)
        send(xe.at[side, pl.ds(core, 1)], hc.at[1 - side, pl.ds(5 - 5 * core, 1)], X_COLS, t_off * 2 + 1 - core, to_h)

    fetches[2].wait()
    fetches[3].wait()
    arrived(STATS2, st2.at[pl.ds(0, 15)])
    first_four = lax.rem(lax.broadcasted_iota(jnp.int32, (4, 128), 1), 8) < 4
    sums = jnp.broadcast_to(jnp.sum(st2[...], axis=0), (4, 128))
    stats = group_totals(jnp.where(jnp.logical_and(mine, first_four), sums, 0.0)) / NUMBERS
    mean = jnp.concatenate([stats[0:1], stats[1:2]], axis=1)
    square = jnp.concatenate([stats[2:3], stats[3:4]], axis=1)
    inverse = lax.rsqrt(square - mean * mean + EPSILON)
    scale, shift = inverse * gain[...], bias[...]

    def activate(v):
        shifted = (v - mean) * scale + shift
        return shifted * jax.nn.sigmoid(shifted)

    arrived(X_PAIR, xraw.at[:, pl.ds(0, 2)])
    for j in range(1, 5):
        act = activate(xraw[:, j].astype(F32).reshape(128, 256))
        acts[1, 2:10, j] = act.astype(BF16).reshape(8, 16, 256)

    turned = jnp.transpose(acts[1, 2:10, 1:5].reshape(512, 256))
    a_t[...] = turned.reshape(8, 2, 16, 512)

    zhi, x_at, zlo, y_at = t // 4, lax.rem(t, 4), h // 4, lax.rem(h, 4)
    z_at = 2 * zhi + zlo

    def products(first, count, keep):
        lhs = a_t[:, core].reshape(128, 512)
        for tap in range(first, first + count, 2):
            taps = range(tap, min(tap + 2, first + count))
            rhs = [s_buf[n % 9, 2 - n // 9 : 10 - n // 9].reshape(512, 128) for n in taps]
            rhs = jnp.concatenate(rhs, axis=1) if len(rhs) == 2 else rhs[0]
            out = jnp.dot(lhs, rhs, preferred_element_type=F32).astype(BF16)
            for i, n in enumerate(taps):
                keep(n - first, out[:, 128 * i : 128 * i + 128].reshape(8, 16, 128))

    def keep_x(n, tiles):
        for z in range(2):
            gx[:, 8 * z + n] = tiles[4 * z : 4 * z + 4]

    def keep_y(n, tiles):
        gy[n % 4, 8 * (n // 4) : 8 * (n // 4) + 8] = tiles

    def keep_z(n, tiles):
        for z in range(2):
            for x in range(4):
                gz[2 * z + n // 4, 4 * x + n % 4] = tiles[4 * z + x]

    def keep_extra(n, tiles):
        for to in range(4):
            if n == 0:
                first, second = to, to + 4
            elif n == 1:
                first, second = (to + 1) % 4, (to + 1) % 4 + 4
            else:
                first = 4 * (to // 2) + 2 * (to // 2 == to % 2)
                second = first + 1
            (gx, gy, gz)[n][to, 16] = tiles[first]
            (gx, gy, gz)[n][to, 17] = tiles[second]

    far = (2, 1, 3)
    products(24, 3, keep_extra)
    products(0, 8, keep_x)
    for k in far:
        to = lax.rem(x_at + k, 4)
        send(gx.at[to], rx.at[x_at], ALONG_X, (zhi * 4 + to) * 2 + core, h)
    products(8, 8, keep_y)
    for k in far:
        to = lax.rem(y_at + k, 4)
        send(gy.at[to], ry.at[y_at], ALONG_Y, tm, zlo * 4 + to)
    products(16, 8, keep_z)
    for k in far:
        to = lax.rem(z_at + k, 4)
        send(gz.at[to], rz.at[z_at], ALONG_Z, (to // 2 * 4 + x_at) * 2 + core, lax.rem(to, 2) * 4 + y_at)
    rx[x_at] = gx[x_at]
    ry[y_at] = gy[y_at]
    rz[z_at] = gz[z_at]
    fetches[4].wait()
    grad = jnp.zeros((256, 256), F32)
    for first in range(0, 27, 2):
        taps = range(first, min(first + 2, 27))
        lhs = [s_buf[n % 9, 2 - n // 9 : 10 - n // 9, pl.ds(2 * core, 2)].reshape(256, 128) for n in taps]
        rhs = [w[n] for n in taps]
        if len(lhs) == 2:
            lhs, rhs = [jnp.concatenate(lhs, axis=1)], [jnp.concatenate(rhs, axis=1)]
        grad = grad + lax.dot_general(lhs[0], rhs[0], (((1,), (1,)), ((), ())), preferred_element_type=F32)

    normed = (xraw[:, pl.ds(1 + 2 * core, 2)].astype(F32).reshape(256, 256) - mean) * inverse
    shifted = normed * gain[...] + shift
    sig = jax.nn.sigmoid(shifted)
    grad = grad * sig * (1.0 + shifted * (1.0 - sig))
    d_gain = jnp.sum(grad * normed, axis=0, keepdims=True)
    d_bias = jnp.sum(grad, axis=0, keepdims=True)
    af[...] = jnp.concatenate([d_gain[:, :128], d_gain[:, 128:], d_bias[:, :128], d_bias[:, 128:]], axis=0)

    for to_h in others_h():
        send(af, at1.at[h], AFF1, tm, to_h)

    at1[h] = af[...]


    @pl.loop(0, 48)
    def _(step):
        a = step // 16
        rows = pl.ds(pl.multiple_of(lax.rem(step, 16) * 16, 16), 16)
        taps = [[w[a * 9 + b * 3 + e, rows, :].astype(F32) for e in range(3)] for b in range(3)]
        for rc, bs in enumerate(((0,), (1, 2), (0, 1), (2,))):
            line = [taps[bs[0]][e] if len(bs) == 1 else taps[bs[0]][e] + taps[bs[1]][e] for e in range(3)]
            for cc, value in enumerate((line[0], line[1] + line[2], line[0] + line[1], line[2])):
                wc[a, rc, rows, 128 * cc : 128 * cc + 128] = value.astype(BF16)

    acts[:, 0:2] = jnp.zeros((3, 2, 6, 16, 256), BF16)
    arrived(X_ROWS, xraw.at[:, pl.ds(0, 1)])
    arrived(X_COLS, hc.at[:, pl.ds(0, 4)])
    border = 5 * core
    inside = jnp.where(core == 0, t > 0, t < CHIPS - 1)
    act = jnp.where(inside, activate(xraw[:, border].astype(F32).reshape(128, 256)), 0.0)
    acts[1, 2:10, border] = act.astype(BF16).reshape(8, 16, 256)
    pads = (pad0, pad1)

    @pl.loop(0, 4)
    def _(k):
        j = 2 * core + k
        here = jnp.logical_or(j != border, inside)
        act = acts[1, 2:10, j].astype(F32).reshape(128, 256)
        act_l = jnp.where(jnp.logical_and(here, h > 0), activate(hc[0, j]), 0.0)
        act_r = jnp.where(jnp.logical_and(here, h < HEIGHT - 1), activate(hc[1, j]), 0.0)
        for half in range(2):
            lanes = slice(128 * half, 128 * half + 128)
            pad = pads[half]
            for f in range(8):
                pad[32 * f + 8 : 32 * f + 24, :] = act[16 * f : 16 * f + 16, lanes]
            pad[pl.ds(7, 8, stride=32), :] = act_l[:, lanes]
            pad[pl.ds(24, 8, stride=32), :] = act_r[:, lanes]
            for f in range(8):
                acts[0, 2 + f, j, :, lanes] = pad[32 * f + 7 : 32 * f + 23, :].astype(BF16)
                acts[2, 2 + f, j, :, lanes] = pad[32 * f + 9 : 32 * f + 25, :].astype(BF16)

    def total_of(parts):
        return jnp.sum(parts[...].astype(F32), axis=0).astype(BF16)

    arrived(ALONG_X, rx.at[pl.ds(0, 3)])
    px[...] = total_of(rx)
    for dz in (1, 0):
        for k in (6, 2, 5, 7, 1, 3, 4, 0):
            if dz or k:
                to_z, to_h = lax.rem(zhi + dz, 2), lax.rem(h + k, 8)
                send(px.at[to_z * 8 + to_h], qx.at[zhi * 8 + h], LAST_X, (to_z * 4 + x_at) * 2 + core, to_h)
    arrived(ALONG_Y, ry.at[pl.ds(0, 3)])
    py[...] = total_of(ry)
    for dz in (1, 0):
        for k in (6, 2, 5, 7, 1, 3, 4, 0):
            if dz or k:
                to_z, to_t = lax.rem(zlo + dz, 2), lax.rem(t + k, 8)
                send(py.at[to_z * 8 + to_t], qy.at[zlo * 8 + t], LAST_Y, to_t * 2 + core, to_z * 4 + y_at)
    arrived(ALONG_Z, rz.at[pl.ds(0, 3)])
    pz[...] = total_of(rz)
    for dx in (2, 1, 3, 0):
        for dy in (2, 1, 3, 0):
            if dx or dy:
                to_x, to_y = lax.rem(x_at + dx, 4), lax.rem(y_at + dy, 4)
                send(pz.at[to_x * 4 + to_y], qz.at[x_at * 4 + y_at], LAST_Z, (zhi * 4 + to_x) * 2 + core, zlo * 4 + to_y)

    def extra(tile, at, to_t, to_h):
        here = jnp.logical_and(to_t == t, to_h == h)

        @pl.when(jnp.logical_not(here))
        def _():
            send(tile, qe.at[at], LAST_E, to_t * 2 + core, to_h)

        @pl.when(here)
        def _():
            qe[at] = tile[...]

    for i in range(2):
        to_t = 4 * i + x_at
        extra(px.at[16 + i], zhi * 8 + h, to_t, to_t)
        to_t = 4 * i + lax.rem(y_at + 1, 4)
        extra(py.at[16 + i], zlo * 8 + t, to_t, lax.rem(to_t + EXTRA[1], 8))
        to_t = 4 * zhi + jnp.where(zhi == zlo, 2, 0) + i
        extra(pz.at[16 + i], x_at * 4 + y_at, to_t, lax.rem(to_t + EXTRA[2], 8))
    qx[zhi * 8 + h] = px[zhi * 8 + h]
    qy[zlo * 8 + t] = py[zlo * 8 + t]
    qz[x_at * 4 + y_at] = pz[x_at * 4 + y_at]

    arrived(AFF1, at1.at[pl.ds(0, 7)])
    at[...] = jnp.sum(at1[...], axis=0)

    for to_tm in others_tm():
        send(at, at2.at[tm], AFF2, to_tm, h)

    at2[tm] = at[...]

    for p in range(2):
        even = jnp.zeros((256, 128), F32)
        odd = jnp.zeros((256, 128), F32)
        for rc, dr in ((0, -1), (1, 0)) if p == 0 else ((2, 0), (3, 1)):
            for a in range(3):
                lhs = [acts[dc, a : a + 8, pl.ds(2 * core + 1 + dr, 2)].reshape(256, 256) for dc in range(3)]
                both = jnp.dot(lhs[1], wc[a, rc, :, 128:384], preferred_element_type=F32)
                even = even + both[:, :128] + jnp.dot(lhs[0], wc[a, rc, :, 0:128], preferred_element_type=F32)
                odd = odd + both[:, 128:] + jnp.dot(lhs[2], wc[a, rc, :, 384:512], preferred_element_type=F32)
        for f in range(8):
            for row in range(2):
                at_row = (f * 4 + 2 * row + p) * 32
                here = (f * 2 + row) * 16
                d_buf[pl.ds(at_row, 16, stride=2), :] = even[here : here + 16]
                d_buf[pl.ds(at_row + 1, 16, stride=2), :] = odd[here : here + 16]
    dec[...] = d_buf[0:1024, :].astype(BF16).reshape(8, 4, 32, 128)

    owners = [lax.rem(t + shift_h, 8) for shift_h in EXTRA]
    has_extra = jnp.logical_or(h == owners[0], jnp.logical_or(h == owners[1], h == owners[2]))
    for i, (kind, parts) in enumerate(((LAST_X, qx), (LAST_Y, qy), (LAST_Z, qz))):
        arrived(kind, parts.at[pl.ds(0, 15)])
        ag_s[i] = total_of(parts)

    @pl.when(has_extra)
    def _():
        arrived(LAST_E, qe.at[pl.ds(0, 15)])
        ag_s[3] = total_of(qe)

    @pl.when(jnp.logical_not(has_extra))
    def _():
        ag_s[3] = jnp.zeros((16, 128), BF16)

    for to_h in others_h():
        send(ag_s, ag_r.at[h], GATHER, tm, to_h)

    ag_r[h] = ag_s[...]

    arrived(AFF2, at2.at[pl.ds(0, 15)])
    total = jnp.sum(at2[...], axis=0)
    aff[0:1, 0:128] = total[0:1]
    aff[0:1, 128:256] = total[1:2]
    aff[1:2, 0:128] = total[2:3]
    aff[1:2, 128:256] = total[3:4]

    arrived(GATHER, ag_r.at[pl.ds(0, 7)])
    for k in range(8):
        for i in range(3):
            gw[8 * i + k] = ag_r[k, i].astype(F32)
    for i in range(3):
        gw[24 + i] = ag_r[owners[i], 3].astype(F32)

    sent(BLOCKS, xraw.at[pl.ds(0, 7), pl.ds(0, 2)])
    sent(COT_PAIR, cpart)
    sent(COT_ROWS, cedge.at[0])
    sent(COT_COLS, ch.at[:, pl.ds(0, 5)])
    sent(ROWS_ON, cedge.at[0])
    sent(COLS_ON, ch.at[:, pl.ds(0, 5)])
    sent(X_PAIR, xraw.at[:, pl.ds(0, 2)])
    sent(X_ROWS, xraw.at[:, pl.ds(0, 1)])
    sent(X_COLS, hc.at[:, pl.ds(0, 4)])
    for kind, parts in ((ALONG_X, rx), (ALONG_Y, ry), (ALONG_Z, rz)):
        sent(kind, parts.at[pl.ds(0, 3)])
    for kind, parts in ((LAST_X, qx), (LAST_Y, qy), (LAST_Z, qz)):
        sent(kind, parts.at[pl.ds(0, 15)])
    sent(LAST_E, qe.at[pl.ds(0, 5)])

    @pl.when(jnp.logical_not(has_extra))
    def _():
        sent(LAST_E, qe.at[0])

    sent(GATHER, ag_r.at[pl.ds(0, 7)])
    sent(STATS1, st1.at[pl.ds(0, 7)])
    sent(STATS2, st2.at[pl.ds(0, 15)])
    sent(AFF1, at1.at[pl.ds(0, 7)])
    sent(AFF2, at2.at[pl.ds(0, 15)])


def deliver(*refs):
    copies = [pltpu.make_async_copy(refs[i], refs[3 + i], refs[6].at[i]) for i in range(3)]
    for copy in copies:
        copy.start()
    for copy in copies:
        copy.wait()


def per_device(coarse, gain, bias, weight, cotangent):
    taps = jnp.transpose(weight, (1, 2, 3, 0, 4)).reshape(27, 256, 128)
    vmem = pl.BlockSpec(memory_space=pltpu.VMEM)
    vm = pltpu.VMEM
    decoded, grad_weight, grad_affine = pl.pallas_call(
        kernel,
        out_shape=(
            jax.ShapeDtypeStruct((8, 4, 32, 128), BF16),
            jax.ShapeDtypeStruct((27, 16, 128), F32),
            jax.ShapeDtypeStruct((2, 256), F32),
        ),
        in_specs=[pl.BlockSpec(memory_space=pltpu.HBM)] * 5,
        out_specs=(vmem, vmem, vmem),
        scratch_shapes=[
            vm((2, 128, 256), BF16),
            vm((1, 256), F32),
            vm((1, 256), F32),
            vm((27, 256, 128), BF16),
            vm((8, 4, 32, 128), BF16),
            pltpu.SemaphoreType.DMA((5,)),
            vm((3, 4, 256, 512), BF16),
            vm((1, 128), F32),
            vm((1, 128), F32),
            vm((8, 1, 128), F32),
            vm((16, 1, 128), F32),
            vm((4, 128), F32),
            vm((4, 128), F32),
            vm((8, 4, 128), F32),
            vm((16, 4, 128), F32),
            vm((8, 6, 16, 256), BF16),
            vm((2, 144, 128), F32),
            vm((2, 2, 8, 256), F32),
            vm((2, 6, 8, 256), F32),
            vm((3, 10, 6, 16, 256), BF16),
            vm((288, 128), F32),
            vm((288, 128), F32),
            vm((8, 2, 16, 512), BF16),
            vm((8, 4, 32, 128), BF16),
            vm((2, 8, 1, 32, 128), BF16),
            vm((2, 4, 8, 128), F32),
            vm((2, 10, 8, 128), F32),
            vm((10 * 8 * 48 + 64, 128), F32),
            vm((9, 10, 4, 16, 128), BF16),
            *[vm((4, 18, 16, 128), BF16)] * 6,
            *[vm((18, 16, 128), BF16)] * 3,
            *[vm((16, 16, 128), BF16)] * 4,
            vm((4, 16, 128), BF16),
            vm((8, 4, 16, 128), BF16),
            vm((1056, 128), F32),
            pltpu.SemaphoreType.DMA((21,)),
            pltpu.SemaphoreType.DMA((21,)),
        ],
        compiler_params=pltpu.CompilerParams(
            collective_id=0, has_side_effects=True, vmem_limit_bytes=48 * 2**20
        ),
        cost_estimate=pl.CostEstimate(flops=2 * 10**9, bytes_accessed=4 * 10**6, transcendentals=300000),
    )(*[
        pltpu.with_memory_space_constraint(x, pltpu.HBM)
        for x in (coarse.reshape(2, 128, 256), gain.reshape(1, 256), bias.reshape(1, 256), taps, cotangent)
    ])
    decoded, grad_weight, grad_affine = pl.pallas_call(
        deliver,
        out_shape=(
            jax.ShapeDtypeStruct((8, 4, 32, 128), BF16),
            jax.ShapeDtypeStruct((27, 16, 128), F32),
            jax.ShapeDtypeStruct((2, 256), F32),
        ),
        in_specs=[pl.BlockSpec(memory_space=pltpu.VMEM)] * 3,
        out_specs=[pl.BlockSpec(memory_space=pl.ANY)] * 3,
        scratch_shapes=[pltpu.SemaphoreType.DMA((3,))],
        compiler_params=pltpu.CompilerParams(vmem_limit_bytes=8 * 2**20),
    )(decoded, grad_weight, grad_affine)
    grad_weight = jnp.transpose(grad_weight.reshape(3, 3, 3, 16, 128), (3, 0, 1, 2, 4))
    return decoded, grad_weight, grad_affine


def solution(mesh):
    return jax.shard_map(
        per_device,
        mesh=mesh,
        in_specs=(P("height", "tm", None, None), P(), P(), P(), P(None, "tm", "height", None)),
        out_specs=(P(None, "tm", "height", None), P("tm", None, None, None, None), P()),
        check_vma=False,
    )
```

profile of v0, /device:TPU:0, one launch (start us, length us, event | category | flops | bytes accessed | tf_op | source)
XLA Modules:
  0.0 34.9 jit_solution(2931231080241751118)
XLA Ops:
  0.6 33.5 %shard_map.76 = (bf16[8,4,32,128]{3,2,1,0:T(8,128)(2,1)S(1)}, f32[27,16,128]{2,1,0:T(8,128)S(1)}, f32[2,256]{1,0:T(2,128)S(1)}) custom-call(bf16[2,128,256]{2,1,0:T(8,128)(2,1)} %bitcast.11, f32[1,256]{1,0:T(1,128)} %bitcast.12, f32[1,256]{1,0:T(1,128)} %bitcast.13, bf16[27,256,128]{2,1,0:T(8,128)(2,1)} %bitcast.9, bf16[8,4,32,128]{3,2,1,0:T(8,128)(2,1)} %cot_hbm.1), custom_call_target="tpu_custom_call" | custom-call | flops 2000000000 | bytes 4000000 | tf_op jit(solution)/shard_map/pallas_call | solution.py:476
  34.1 0.8 %shard_map.77 = (bf16[8,4,32,128]{3,2,1,0:T(8,128)(2,1)}, f32[27,16,128]{2,1,0:T(8,128)}, f32[2,256]{1,0:T(2,128)}) custom-call(bf16[8,4,32,128]{3,2,1,0:T(8,128)(2,1)S(1)} %get-tuple-element.9.refs_0_, f32[27,16,128]{2,1,0:T(8,128)S(1)} %get-tuple-element.10.refs_1_, f32[2,256]{1,0:T(2,128)S(1)} %get-tuple-element.11.refs_2_), custom_call_target="tpu_custom_call" | custom-call | tf_op jit(solution)/shard_map/pallas_call | solution.py:532
where the time goes:
time: 35.1 us; the launch traced here: 34.9 us
  Pallas kernels  34.3 us (98%)
  between operations  0.64 us (2%)
    pallas_call x1, Pallas kernels, per_device(): pl.pallas_call(kernel, out_shape=(jax.ShapeDtypeStruct((8, 4, 32, 128), B...  33.5 us
    pallas_call x1, Pallas kernels, per_device(): pl.pallas_call(deliver, out_shape=(jax.ShapeDtypeStruct((8, 4, 32, 128),...  0.8 us

commit v1 on v0

--- a/solution.py
+++ b/solution.py
@@ -14,7 +14,7 @@
 CHIPS, HEIGHT = 8, 8
 EXTRA = (0, 3, 6)
 
-(STATS1, STATS2, BLOCKS, COT_PAIR, COT_ROWS, COT_COLS, X_PAIR, X_ROWS, X_COLS, ALONG_X, ALONG_Y, ALONG_Z, LAST_X, LAST_Y, LAST_Z, LAST_E, GATHER, AFF1, AFF2, ROWS_ON, COLS_ON) = range(21)
+(STATS1, STATS2, BLOCKS, COT_PAIR, COT_ROWS, COT_COLS, X_PAIR, X_ROWS, X_COLS, ALONG_X, ALONG_Y, ALONG_Z, LAST_X, LAST_Y, LAST_Z, LAST_E, GATHER, AFF1, AFF2, ROWS_ON, COLS_ON, X_COLS_ON) = range(22)
 
 
 def group_totals(tile):
@@ -79,14 +79,8 @@
     for to_h in others_h():
         greet(tm, to_h)
 
-    greet(pair, left)
-    greet(pair, right)
-
-    @pl.loop(0, 4)
-    def _(k):
-        to_tm = lax.rem(t + 7 + 2 * (k // 2), 8) * 2 + lax.rem(k, 2)
-        greet(to_tm, left)
-        greet(to_tm, right)
+    for to_h in (left, right):
+        greet(t_off * 2 + 1 - core, to_h)
 
     fetches[0].wait()
     x = coarse[...].astype(F32).reshape(256, 256)
@@ -98,7 +92,7 @@
     sums = group_totals(jnp.concatenate(quarters, axis=0))
     st[...] = jnp.sum(jnp.where(mine, sums, 0.0), axis=0, keepdims=True)
 
-    pl.semaphore_wait(barrier, 32)
+    pl.semaphore_wait(barrier, 24)
 
     for to_h in others_h():
         send(st, st1.at[h], STATS1, tm, to_h)
@@ -188,7 +182,6 @@
                 xe[side, r, :, 128 * half : 128 * half + 128] = xf.at[half][pl.ds(column, 8, stride=16), :]
     for side, to_h in ((0, left), (1, right)):
         send(xe.at[side], hc.at[1 - side, pl.ds(1 + 2 * core, 2)], X_COLS, tm, to_h)
-        send(xe.at[side, pl.ds(1 - core, 1)], hc.at[1 - side, pl.ds(2 + core, 1)], X_COLS, pair, to_h)
         send(xe.at[side, pl.ds(core, 1)], hc.at[1 - side, pl.ds(5 - 5 * core, 1)], X_COLS, t_off * 2 + 1 - core, to_h)
 
     fetches[2].wait()
@@ -291,6 +284,10 @@
 
     at1[h] = af[...]
 
+    arrived(X_COLS, hc.at[:, pl.ds(0, 3)])
+    next_to_pair = hc.at[:, pl.ds(2 + core, 1)]
+    send(next_to_pair, next_to_pair, X_COLS_ON, pair, h)
+
 
     @pl.loop(0, 48)
     def _(step):
@@ -304,7 +301,7 @@
 
     acts[:, 0:2] = jnp.zeros((3, 2, 6, 16, 256), BF16)
     arrived(X_ROWS, xraw.at[:, pl.ds(0, 1)])
-    arrived(X_COLS, hc.at[:, pl.ds(0, 4)])
+    arrived(X_COLS_ON, hc.at[:, pl.ds(0, 1)])
     border = 5 * core
     inside = jnp.where(core == 0, t > 0, t < CHIPS - 1)
     act = jnp.where(inside, activate(xraw[:, border].astype(F32).reshape(128, 256)), 0.0)
@@ -443,7 +440,8 @@
     sent(COLS_ON, ch.at[:, pl.ds(0, 5)])
     sent(X_PAIR, xraw.at[:, pl.ds(0, 2)])
     sent(X_ROWS, xraw.at[:, pl.ds(0, 1)])
-    sent(X_COLS, hc.at[:, pl.ds(0, 4)])
+    sent(X_COLS, hc.at[:, pl.ds(0, 3)])
+    sent(X_COLS_ON, hc.at[:, pl.ds(0, 1)])
     for kind, parts in ((ALONG_X, rx), (ALONG_Y, ry), (ALONG_Z, rz)):
         sent(kind, parts.at[pl.ds(0, 3)])
     for kind, parts in ((LAST_X, qx), (LAST_Y, qy), (LAST_Z, qz)):
@@ -518,8 +516,8 @@
             vm((4, 16, 128), BF16),
             vm((8, 4, 16, 128), BF16),
             vm((1056, 128), F32),
-            pltpu.SemaphoreType.DMA((21,)),
-            pltpu.SemaphoreType.DMA((21,)),
+            pltpu.SemaphoreType.DMA((22,)),
+            pltpu.SemaphoreType.DMA((22,)),
         ],
         compiler_params=pltpu.CompilerParams(
             collective_id=0, has_side_effects=True, vmem_limit_bytes=48 * 2**20

time: 35.1 us -> 34.4 us (0.980)
  Pallas kernels: 34.3 us -> 33.6 us
    pallas_call x1, Pallas kernels: 33.5 us -> 32.8 us  [per_device(): pl.pallas_call(kernel, out_shape=(jax.ShapeDtypeStruct((8, 4, 32, 128), B...]
where the time goes in v1:
time: 34.4 us; the launch traced here: 34.2 us
  Pallas kernels  33.6 us (98%)
  between operations  0.64 us (2%)
    pallas_call x1, Pallas kernels, per_device(): pl.pallas_call(kernel, out_shape=(jax.ShapeDtypeStruct((8, 4, 32, 128), B...  32.8 us
    pallas_call x1, Pallas kernels, per_device(): pl.pallas_call(deliver, out_shape=(jax.ShapeDtypeStruct((8, 4, 32, 128),...  0.8 us

profile of v1, /device:TPU:0, one launch (start us, length us, event | category | flops | bytes accessed | tf_op | source)
XLA Modules:
  0.0 34.2 jit_solution(8944984488629902263)
XLA Ops:
  0.6 32.8 %shard_map.76 = (bf16[8,4,32,128]{3,2,1,0:T(8,128)(2,1)S(1)}, f32[27,16,128]{2,1,0:T(8,128)S(1)}, f32[2,256]{1,0:T(2,128)S(1)}) custom-call(bf16[2,128,256]{2,1,0:T(8,128)(2,1)} %bitcast.11, f32[1,256]{1,0:T(1,128)} %bitcast.12, f32[1,256]{1,0:T(1,128)} %bitcast.13, bf16[27,256,128]{2,1,0:T(8,128)(2,1)} %bitcast.9, bf16[8,4,32,128]{3,2,1,0:T(8,128)(2,1)} %cot_hbm.1), custom_call_target="tpu_custom_call" | custom-call | flops 2000000000 | bytes 4000000 | tf_op jit(solution)/shard_map/pallas_call | solution.py:474
  33.4 0.8 %shard_map.77 = (bf16[8,4,32,128]{3,2,1,0:T(8,128)(2,1)}, f32[27,16,128]{2,1,0:T(8,128)}, f32[2,256]{1,0:T(2,128)}) custom-call(bf16[8,4,32,128]{3,2,1,0:T(8,128)(2,1)S(1)} %get-tuple-element.9.refs_0_, f32[27,16,128]{2,1,0:T(8,128)S(1)} %get-tuple-element.10.refs_1_, f32[2,256]{1,0:T(2,128)S(1)} %get-tuple-element.11.refs_2_), custom_call_target="tpu_custom_call" | custom-call | tf_op jit(solution)/shard_map/pallas_call | solution.py:530

commit v2 on v1

--- a/solution.py
+++ b/solution.py
@@ -74,13 +74,13 @@
     def greet(to_tm, to_h):
         pl.semaphore_signal(barrier, inc=1, device_id=(to_tm, to_h), device_id_type=MESH)
 
+    for to_h in (left, right):
+        greet(t_off * 2 + 1 - core, to_h)
     for to_tm in others_tm():
         greet(to_tm, h)
     for to_h in others_h():
         greet(tm, to_h)
 
-    for to_h in (left, right):
-        greet(t_off * 2 + 1 - core, to_h)
 
     fetches[0].wait()
     x = coarse[...].astype(F32).reshape(256, 256)

time: 34.4 us -> 34.3 us (level)
  no operation moved by 1% of the time
where the time goes in v2:
time: 34.3 us; the launch traced here: 34.1 us
  Pallas kernels  33.5 us (98%)
  between operations  0.64 us (2%)
    pallas_call x1, Pallas kernels, per_device(): pl.pallas_call(kernel, out_shape=(jax.ShapeDtypeStruct((8, 4, 32, 128), B...  32.7 us
    pallas_call x1, Pallas kernels, per_device(): pl.pallas_call(deliver, out_shape=(jax.ShapeDtypeStruct((8, 4, 32, 128),...  0.8 us

profile of v2, /device:TPU:0, one launch (start us, length us, event | category | flops | bytes accessed | tf_op | source)
XLA Modules:
  0.0 34.1 jit_solution(15043382067352861906)
XLA Ops:
  0.6 32.7 %shard_map.76 = (bf16[8,4,32,128]{3,2,1,0:T(8,128)(2,1)S(1)}, f32[27,16,128]{2,1,0:T(8,128)S(1)}, f32[2,256]{1,0:T(2,128)S(1)}) custom-call(bf16[2,128,256]{2,1,0:T(8,128)(2,1)} %bitcast.11, f32[1,256]{1,0:T(1,128)} %bitcast.12, f32[1,256]{1,0:T(1,128)} %bitcast.13, bf16[27,256,128]{2,1,0:T(8,128)(2,1)} %bitcast.9, bf16[8,4,32,128]{3,2,1,0:T(8,128)(2,1)} %cot_hbm.1), custom_call_target="tpu_custom_call" | custom-call | flops 2000000000 | bytes 4000000 | tf_op jit(solution)/shard_map/pallas_call | solution.py:474
  33.3 0.8 %shard_map.77 = (bf16[8,4,32,128]{3,2,1,0:T(8,128)(2,1)}, f32[27,16,128]{2,1,0:T(8,128)}, f32[2,256]{1,0:T(2,128)}) custom-call(bf16[8,4,32,128]{3,2,1,0:T(8,128)(2,1)S(1)} %get-tuple-element.9.refs_0_, f32[27,16,128]{2,1,0:T(8,128)S(1)} %get-tuple-element.10.refs_1_, f32[2,256]{1,0:T(2,128)S(1)} %get-tuple-element.11.refs_2_), custom_call_target="tpu_custom_call" | custom-call | tf_op jit(solution)/shard_map/pallas_call | solution.py:530

commit v3 on v2

--- a/solution.py
+++ b/solution.py
@@ -97,12 +97,6 @@
     for to_h in others_h():
         send(st, st1.at[h], STATS1, tm, to_h)
 
-    for to_h in others_h():
-        send(
-            coarse.at[:, pl.ds(pl.multiple_of(to_h * 16, 16), 16), :],
-            xraw.at[h, pl.ds(1 + 2 * core, 2)], BLOCKS, tm, to_h,
-        )
-
     fetches[1].wait()
     send(cot, cpart, COT_PAIR, pair, h)
     send(cot.at[:, pl.ds(3 * core, 1)], cedge.at[1 - core], COT_ROWS, t_off * 2 + 1 - core, h)
@@ -120,6 +114,12 @@
     for side, to_h in ((0, left), (1, right)):
         send(ce.at[side], ch.at[1 - side, pl.ds(1 + 4 * core, 4)], COT_COLS, tm, to_h)
         send(ce.at[side, pl.ds(3 * core, 1)], ch.at[1 - side, pl.ds(9 - 9 * core, 1)], COT_COLS, t_off * 2 + 1 - core, to_h)
+
+    for to_h in others_h():
+        send(
+            coarse.at[:, pl.ds(pl.multiple_of(to_h * 16, 16), 16), :],
+            xraw.at[h, pl.ds(1 + 2 * core, 2)], BLOCKS, tm, to_h,
+        )
 
     st1[h] = st[...]
     xraw[h, pl.ds(1 + 2 * core, 2)] = coarse[:, pl.ds(pl.multiple_of(h * 16, 16), 16), :]

time: 34.3 us -> 34.1 us (level)
  no operation moved by 1% of the time
where the time goes in v3:
time: 34.1 us; the launch traced here: 34 us
  Pallas kernels  33.3 us (98%)
  between operations  0.64 us (2%)
    pallas_call x1, Pallas kernels, per_device(): pl.pallas_call(kernel, out_shape=(jax.ShapeDtypeStruct((8, 4, 32, 128), B...  32.5 us
    pallas_call x1, Pallas kernels, per_device(): pl.pallas_call(deliver, out_shape=(jax.ShapeDtypeStruct((8, 4, 32, 128),...  0.8 us

profile of v3, /device:TPU:0, one launch (start us, length us, event | category | flops | bytes accessed | tf_op | source)
XLA Modules:
  0.0 34.0 jit_solution(3580615074564207802)
XLA Ops:
  0.6 32.5 %shard_map.76 = (bf16[8,4,32,128]{3,2,1,0:T(8,128)(2,1)S(1)}, f32[27,16,128]{2,1,0:T(8,128)S(1)}, f32[2,256]{1,0:T(2,128)S(1)}) custom-call(bf16[2,128,256]{2,1,0:T(8,128)(2,1)} %bitcast.11, f32[1,256]{1,0:T(1,128)} %bitcast.12, f32[1,256]{1,0:T(1,128)} %bitcast.13, bf16[27,256,128]{2,1,0:T(8,128)(2,1)} %bitcast.9, bf16[8,4,32,128]{3,2,1,0:T(8,128)(2,1)} %cot_hbm.1), custom_call_target="tpu_custom_call" | custom-call | flops 2000000000 | bytes 4000000 | tf_op jit(solution)/shard_map/pallas_call | solution.py:474
  33.2 0.8 %shard_map.77 = (bf16[8,4,32,128]{3,2,1,0:T(8,128)(2,1)}, f32[27,16,128]{2,1,0:T(8,128)}, f32[2,256]{1,0:T(2,128)}) custom-call(bf16[8,4,32,128]{3,2,1,0:T(8,128)(2,1)S(1)} %get-tuple-element.9.refs_0_, f32[27,16,128]{2,1,0:T(8,128)S(1)} %get-tuple-element.10.refs_1_, f32[2,256]{1,0:T(2,128)S(1)} %get-tuple-element.11.refs_2_), custom_call_target="tpu_custom_call" | custom-call | tf_op jit(solution)/shard_map/pallas_call | solution.py:530
